TPU v7x, 32 devices: a whole 2x2x4 slice. The times are simulated.
32 devices in a mesh: grp: 2 (over y), sp: 4 (over z), flt: 2 (over x), rep: 2 (over core).
Axes of the slice: x: 2, y: 2, z: 4, core: 2. Of those that a mesh axis runs over, the one named last changes fastest.
Arguments:
- acts: float32 [64, 8, 8, 512], P(None, ('grp', 'sp'), ('flt', 'rep')), parts along dimension 1, may hold values from -6 to 6
- grad_out: float32 [64, 8, 8, 512], P(None, ('grp', 'sp'), ('flt', 'rep')), parts along dimension 1, may hold values from -6 to 6
- kernel: float32 [3, 3, 3, 64, 64], replicated, may hold values from -0.15625 to 0.15625
Outputs:
- input_grad: float32 [64, 8, 8, 512], P(None, ('grp', 'sp'), ('flt', 'rep')), parts along dimension 1
- weight_grad: float32 [6, 3, 3, 64, 64], P('grp'), parts along dimension 0
There are 2 independent parts, one for each index of `grp`. A program takes and returns all parts, laid end to end along the dimension named above; an argument that names none is the same for every part. Nothing has to cross between parts.
All inputs are finite; a program needn't handle non-finite values.
Results may differ from a plain program's by a relative error of at most 0.00007.
Values sent between devices are 32-bit elements; how exact they have to be, the bound alone decides.
A program may use at most 64 MiB of HBM per device.

v0:
```python
import math

import jax
import jax.numpy as jnp
from jax import lax
from jax.sharding import PartitionSpec as P


def padded_2(value, sides, width):
    for axis, dim in sides:
        count, length = (lax.axis_size(axis), value.shape[dim])
        up = [(i, (i + 1) % count) for i in range(count - 1)]
        down = [(j, i) for i, j in up]
        last = lax.slice_in_dim(value, length - width, length, axis=dim)
        first = lax.slice_in_dim(value, 0, width, axis=dim)
        before = lax.ppermute(last, axis, up)
        after = lax.ppermute(first, axis, down)
        value = jnp.concatenate([before, value, after], axis=dim)
    return value


def take_next(values):
    edge = jnp.zeros(values.shape[:-1] + (1,), values.dtype)
    return jnp.concatenate([values[..., 1:], edge], axis=-1)


def take_prior(values):
    edge = jnp.zeros(values.shape[:-1] + (1,), values.dtype)
    return jnp.concatenate([edge, values[..., :-1]], axis=-1)


def contract_last(left, right):
    return lax.dot_general(left, right, (((1,), (1,)), ((), ())), precision=lax.Precision.HIGHEST)


def per_device(acts, grad_out, kernel):
    cin = acts.shape[0]
    planes = acts.shape[1]
    rows = acts.shape[2]
    width = acts.shape[3]
    cout = grad_out.shape[0]
    voxels = (
        planes * lax.axis_size("sp") * rows * lax.axis_size("flt") * lax.axis_size("rep") * width
    )
    factor = 1.0 / math.sqrt(voxels)
    padded = padded_2(grad_out, (("sp", 1), (("flt", "rep"), 2)), 1)
    weights_tap = kernel.reshape(9, 3 * cin, cout)
    weight_terms = [jnp.zeros((3 * cin, cout), jnp.float32) for index in range(9)]
    source = acts[:, 0]
    source_stack = jnp.concatenate([take_prior(source), source, take_next(source)], axis=0).reshape(
        3 * cin, rows * width
    )
    partial_sum = jnp.zeros((3 * cin, rows * width), jnp.float32)
    for a_tap in range(3):
        for b_tap in range(3):
            index = 3 * a_tap + b_tap
            slab = padded[:, 2 - a_tap, 2 - b_tap : 2 - b_tap + rows, :].reshape(cout, rows * width)
            partial_sum = partial_sum + jnp.dot(
                weights_tap[index], slab, precision=lax.Precision.HIGHEST
            )
            weight_terms[index] = contract_last(source_stack, slab)
    parts_x = partial_sum.reshape(3, cin, rows, width)
    plane_out = take_next(parts_x[0]) + parts_x[1] + take_prior(parts_x[2])
    outputs = [plane_out]
    term = jnp.stack(weight_terms, axis=0).reshape(3, 3, 3, cin, cout) * factor
    weight_grad = lax.psum(term, ("sp", "flt", "rep"))
    input_grad = jnp.stack(outputs, axis=1)
    return (input_grad, weight_grad)


def solution(mesh):
    placed = (
        P(None, ("grp", "sp"), ("flt", "rep"), None),
        P(None, ("grp", "sp"), ("flt", "rep"), None),
        P(),
    )
    return jax.shard_map(
        per_device,
        mesh=mesh,
        in_specs=placed,
        out_specs=(P(None, ("grp", "sp"), ("flt", "rep"), None), P("grp", None, None, None, None)),
        check_vma=False,
    )
```

profile of v0, /device:TPU:1, one launch (start us, length us, event | category | flops | bytes accessed | tf_op | source)
XLA Modules:
  0.0 145.9 jit_solution(15860099137105820920)
XLA Ops:
  7.2 1.0 copy.11
  8.2 4.2 %collective-permute-start = (f32[64,1,2,512]{3,0,2,1:T(8,128)S(1)}, f32[64,1,2,512]{3,0,2,1:T(8,128)S(1)}, u32[]{:S(2)}, u32[]{:S(2)}) collective-permute-start(f32[64,1,2,512]{3,0,2,1:T(8,128)S(1)} %copy.11), channel_id=1, source_target_pairs={{0,4},{4,8},{8,12},{1,5},{5,9},{9,13},{2,6},{6,10},{10,14},{3,7},{... | collective-permute-start | bytes 786440 | tf_op jit(solution)/shard_map/ppermute | solution.py:16
  12.4 1.3 collective-permute-start.1
  13.7 3.6 %collective-permute-done = f32[64,1,2,512]{3,0,2,1:T(8,128)S(1)} collective-permute-done((f32[64,1,2,512]{3,0,2,1:T(8,128)S(1)}, f32[64,1,2,512]{3,0,2,1:T(8,128)S(1)}, u32[]{:S(2)}, u32[]{:S(2)}) %collective-permute-start) | collective-permute-done | bytes 262176 | tf_op jit(solution)/shard_map/ppermute | solution.py:16
  17.4 3.7 %collective-permute-done.1 = f32[64,1,2,512]{3,0,2,1:T(8,128)S(1)} collective-permute-done((f32[64,1,2,512]{3,0,2,1:T(8,128)S(1)}, f32[64,1,2,512]{3,0,2,1:T(8,128)S(1)}, u32[]{:S(2)}, u32[]{:S(2)}) %collective-permute-start.1) | collective-permute-done | bytes 262176 | tf_op jit(solution)/shard_map/ppermute | solution.py:17
  21.3 3.8 %collective-permute-start.2 = (f32[64,3,1,512]{3,0,2,1:T(8,128)S(1)}, f32[64,3,1,512]{3,0,2,1:T(8,128)S(1)}, u32[]{:S(2)}, u32[]{:S(2)}) collective-permute-start(f32[64,3,1,512]{3,0,2,1:T(8,128)S(1)} %get-tuple-element.15), channel_id=1, source_target_pairs={{1,0},{2,1},{3,2},{5,4},{6,5},{7,6},{9,8},{10,9},{11,10},{13,12},{... | collective-permute-start | bytes 1179656 | tf_op jit(solution)/shard_map/ppermute | solution.py:17
  25.1 3.0 %collective-permute-start.3 = (f32[64,3,1,512]{3,0,2,1:T(8,128)S(1)}, f32[64,3,1,512]{3,0,2,1:T(8,128)S(1)}, u32[]{:S(2)}, u32[]{:S(2)}) collective-permute-start(f32[64,3,1,512]{3,0,2,1:T(8,128)S(1)} %get-tuple-element.14), channel_id=1, source_target_pairs={{0,1},{1,2},{2,3},{4,5},{5,6},{6,7},{8,9},{9,10},{10,11},{12,13},{... | collective-permute-start | bytes 1179656 | tf_op jit(solution)/shard_map/ppermute | solution.py:16
  28.1 0.3 fusion.16
  28.4 0.3 concatenate.41
  28.9 0.1 concatenate.44
  29.2 0.2 copy.15
  29.5 0.2 copy.20
  29.7 1.9 %collective-permute-done.2 = f32[64,3,1,512]{3,0,2,1:T(8,128)S(1)} collective-permute-done((f32[64,3,1,512]{3,0,2,1:T(8,128)S(1)}, f32[64,3,1,512]{3,0,2,1:T(8,128)S(1)}, u32[]{:S(2)}, u32[]{:S(2)}) %collective-permute-start.2) | collective-permute-done | bytes 393248 | tf_op jit(solution)/shard_map/ppermute | solution.py:17
  31.6 1.2 collective-permute-done.3
  32.8 0.1 pad_maximum_fusion
  32.9 0.2 copy.14
  33.2 0.2 copy.16
  33.4 0.2 copy.17
  33.7 0.2 copy.18
  34.0 0.2 copy.19
  34.3 0.2 copy.21
  34.5 0.9 fusion.13
  35.4 0.9 fusion.12
  36.3 0.9 fusion.11
  37.2 0.9 fusion.10
  38.0 0.9 fusion.9
  38.9 0.9 fusion.8
  39.8 0.9 fusion.7
  40.7 0.9 fusion.6
  41.6 0.9 fusion.5
  42.5 1.2 copy.22
  43.7 1.1 copy-done.2
  44.9 0.8 convolution_bitcast_fusion.5
  45.7 0.8 convolution_add_fusion.2
  46.4 0.8 fusion.4
  47.2 0.8 fusion.3
  48.0 0.9 convolution_add_fusion.1
  48.9 0.8 fusion.2
  49.7 0.8 fusion.1
  50.5 0.8 convolution_add_fusion
  51.3 0.8 fusion
  52.1 0.2 squeeze.48
  52.3 0.3 slice.117
  52.7 0.2 squeeze.50
  52.9 0.2 squeeze.49
  53.1 1.0 add_bitcast_fusion
  54.2 82.7 %all-reduce.6.cloned.1.call-done = f32[3,3,3,64,64]{4,3,2,1,0:T(8,128)} async-done(((f32[3,3,3,64,64]{4,3,2,1,0:T(8,128)}), f32[3,3,3,64,64]{4,3,2,1,0:T(8,128)}) %all-reduce.6.cloned.1.call-update) | async-done | bytes 442384 | tf_op jit(solution)/shard_map/psum | solution.py:66
  136.9 2.2 %copy.49 = f32[3,3,3,64,64]{4,3,2,1,0:T(8,128)} copy(f32[3,3,3,64,64]{4,3,2,1,0:T(8,128)} %all-reduce.6.cloned.1.call-done) | data formatting | bytes 884736
  (28 shorter events, 1.0 us)
Async XLA Ops:
  7.2 129.7 %all-reduce.6.cloned.1.call-start = ((), (), s32[]{:S(2)}) async-start(), calls=%async_computation | async-start | bytes 1769472 | tf_op jit(solution)/shard_map/psum | solution.py:66
  8.2 9.2 %copy-start.1 = (f32[64,1,2,512]{3,2,1,0:T(2,128)S(1)}, f32[64,1,2,512]{3,2,1,0:T(2,128)}, u32[]{:S(2)}) copy-start(f32[64,1,2,512]{3,2,1,0:T(2,128)} %param.4) | copy-start | bytes 786436
  8.2 9.1 %collective-permute-start = (f32[64,1,2,512]{3,0,2,1:T(8,128)S(1)}, f32[64,1,2,512]{3,0,2,1:T(8,128)S(1)}, u32[]{:S(2)}, u32[]{:S(2)}) collective-permute-start(f32[64,1,2,512]{3,0,2,1:T(8,128)S(1)} %copy.11), channel_id=1, source_target_pairs={{0,4},{4,8},{8,12},{1,5},{5,9},{9,13},{2,6},{6,10},{10,14},{3,7},{... | collective-permute-start | bytes 786440 | tf_op jit(solution)/shard_map/ppermute | solution.py:16
  12.4 8.8 %collective-permute-start.1 = (f32[64,1,2,512]{3,0,2,1:T(8,128)S(1)}, f32[64,1,2,512]{3,0,2,1:T(8,128)S(1)}, u32[]{:S(2)}, u32[]{:S(2)}) collective-permute-start(f32[64,1,2,512]{3,0,2,1:T(8,128)S(1)} %copy.11), channel_id=1, source_target_pairs={{4,0},{8,4},{12,8},{5,1},{9,5},{13,9},{6,2},{10,6},{14,10},{7,3},{... | collective-permute-start | bytes 786440 | tf_op jit(solution)/shard_map/ppermute | solution.py:17
  21.2 6.9 %copy-start = (f32[64,1,2,512]{3,2,1,0:T(2,128)S(1)}, f32[64,1,2,512]{3,2,1,0:T(2,128)}, u32[]{:S(2)}) copy-start(f32[64,1,2,512]{3,2,1,0:T(2,128)} %param.3) | copy-start | bytes 786436
  21.3 10.3 %collective-permute-start.2 = (f32[64,3,1,512]{3,0,2,1:T(8,128)S(1)}, f32[64,3,1,512]{3,0,2,1:T(8,128)S(1)}, u32[]{:S(2)}, u32[]{:S(2)}) collective-permute-start(f32[64,3,1,512]{3,0,2,1:T(8,128)S(1)} %get-tuple-element.15), channel_id=1, source_target_pairs={{1,0},{2,1},{3,2},{5,4},{6,5},{7,6},{9,8},{10,9},{11,10},{13,12},{... | collective-permute-start | bytes 1179656 | tf_op jit(solution)/shard_map/ppermute | solution.py:17
  25.1 7.7 %collective-permute-start.3 = (f32[64,3,1,512]{3,0,2,1:T(8,128)S(1)}, f32[64,3,1,512]{3,0,2,1:T(8,128)S(1)}, u32[]{:S(2)}, u32[]{:S(2)}) collective-permute-start(f32[64,3,1,512]{3,0,2,1:T(8,128)S(1)} %get-tuple-element.14), channel_id=1, source_target_pairs={{0,1},{1,2},{2,3},{4,5},{5,6},{6,7},{8,9},{9,10},{10,11},{12,13},{... | collective-permute-start | bytes 1179656 | tf_op jit(solution)/shard_map/ppermute | solution.py:16
  43.7 1.2 copy-start.2
Sparse Core Ops, SparseCore 0:
  43.9 92.9 all-reduce.5
where the time goes:
time: 148 us; the launch traced here: 146 us
  waiting for transfers between devices  93.2 us (63%)
  matrix products  15 us (10%)
  between operations  14.4 us (10%)
  starting transfers between devices  12.3 us (8%)
  local copies, waits for them, and re-layouts  9.81 us (7%)
    psum x1, waiting for transfers between devices, per_device(): weight_grad = lax.psum(term, ('sp', 'flt', 'rep'))  82.7 us
    dot_general x9, matrix products, contract_last(): lax.dot_general(left, right, (((1,), (1,)), ((), ())), precision=lax.Prec...  7.91 us
    ppermute x2, starting transfers between devices, padded_2(): before = lax.ppermute(last, axis, up)  7.19 us
    dot_general x9, matrix products, per_device(): jnp.dot(weights_tap[index], slab, precision=lax.Precision.HIGHEST)  7.09 us
    ppermute x2, waiting for transfers between devices, padded_2(): after = lax.ppermute(first, axis, down)  5.61 us
    ppermute x2, starting transfers between devices, padded_2(): after = lax.ppermute(first, axis, down)  5.07 us
    unnamed x24, local copies, waits for them, and re-layouts  5.03 us
    ppermute x2, waiting for transfers between devices, padded_2(): before = lax.ppermute(last, axis, up)  4.82 us
  transfers between devices with their start and end apart: 5, of which 5 were waited for; matrix products, arithmetic and copies ran while one was open for 7% of the time, Pallas kernels for 0%

commit v1 on v0

--- a/solution.py
+++ b/solution.py
@@ -1,9 +1,189 @@
+import functools
 import math
 
 import jax
 import jax.numpy as jnp
 from jax import lax
+from jax.experimental import pallas as pl
+from jax.experimental.pallas import tpu as pltpu
 from jax.sharding import PartitionSpec as P
+
+MESH = pl.DeviceIdType.MESH
+VMEM = pltpu.VMEM
+
+
+class Group:
+    def __init__(self, sp, flt):
+        self.flt, self.count = flt, sp * flt
+        self.core = lax.axis_index("rep")
+        self.chip = lax.axis_index("sp") * flt + lax.axis_index("flt")
+
+    def peer(self, chip):
+        return {"sp": chip // self.flt, "flt": chip % self.flt}
+
+    def partner(self):
+        return {"rep": 1 - self.core}
+
+    def after(self, step):
+        return lax.rem(self.chip + 1 + step, self.count)
+
+    def before(self, step):
+        return lax.rem(self.chip + 2 * self.count - 1 - step, self.count)
+
+
+def sum_over_group(group, piece, terms, held, arrived, total, sems):
+    core, chip, count = group.core, group.chip, group.count
+    half = count * piece
+
+    def rows(at):
+        return pl.ds(pl.multiple_of(at, 8), piece)
+
+    def to_partner(j):
+        return pltpu.make_async_remote_copy(
+            terms.at[rows((1 - core) * half + j * piece)],
+            held.at[rows(j * piece)],
+            sems.at[0, j],
+            sems.at[1, j],
+            device_id=group.partner(),
+            device_id_type=MESH,
+        )
+
+    def scatter(j, slot):
+        return pltpu.make_async_remote_copy(
+            held.at[rows(j * piece)],
+            arrived.at[rows(slot * piece)],
+            sems.at[2, j],
+            sems.at[3, slot],
+            device_id=group.peer(j),
+            device_id_type=MESH,
+        )
+
+    def gather(j, slot):
+        part = total.at[rows(core * half + slot * piece)]
+        return pltpu.make_async_remote_copy(
+            part,
+            part,
+            sems.at[4, j],
+            sems.at[5, slot],
+            device_id=group.peer(j),
+            device_id_type=MESH,
+        )
+
+    def pass_on(j, owner):
+        part = total.at[rows(owner * half + j * piece)]
+        return pltpu.make_async_remote_copy(
+            part,
+            part,
+            sems.at[6, j],
+            sems.at[7, j],
+            device_id=group.partner(),
+            device_id_type=MESH,
+        )
+
+    def each(steps, body):
+        def run(step, carry):
+            body(step)
+            return carry
+
+        lax.fori_loop(0, steps, run, 0)
+
+    def start():
+        each(count, lambda k: to_partner(group.after(k)).start())
+
+    def add_and_scatter(k):
+        j = group.after(k)
+        to_partner(j).wait_recv()
+        own = rows(j * piece)
+        held[own, :] = held[own, :] + terms[rows(core * half + j * piece), :]
+
+        @pl.when(k < count - 1)
+        def _():
+            scatter(j, chip).start()
+
+    def add_arrived(k):
+        j = group.before(k)
+        scatter(j, j).wait_recv()
+        own = rows(chip * piece)
+        held[own, :] = held[own, :] + arrived[rows(j * piece), :]
+
+    def middle():
+        each(count, add_and_scatter)
+
+    def forward(k):
+        j = group.before(k)
+        gather(j, j).wait_recv()
+        pass_on(j, core).start()
+
+    def finish():
+        each(count - 1, add_arrived)
+        total[rows(core * half + chip * piece), :] = held[rows(chip * piece), :]
+        each(count - 1, lambda k: gather(group.after(k), chip).start())
+        pass_on(chip, core).start()
+        each(count - 1, forward)
+        each(count, lambda k: pass_on(k, 1 - core).wait_recv())
+        each(count, lambda k: to_partner(k).wait_send())
+        each(count, lambda k: pass_on(k, core).wait_send())
+
+        def sent(k):
+            j = group.after(k)
+            scatter(j, chip).wait_send()
+            gather(j, chip).wait_send()
+
+        each(count - 1, sent)
+
+    return start, middle, finish
+
+
+def greet(devices):
+    barrier = pltpu.get_barrier_semaphore()
+    for device in devices:
+        pl.semaphore_signal(barrier, 1, device_id=device, device_id_type=MESH)
+    return barrier
+
+
+def greet_group(group):
+    barrier = greet([group.partner()])
+
+    def run(k, carry):
+        pl.semaphore_signal(
+            barrier, 1, device_id=group.peer(group.after(k)), device_id_type=MESH
+        )
+        return carry
+
+    lax.fori_loop(0, group.count - 1, run, 0)
+    pl.semaphore_wait(barrier, group.count)
+
+
+def reduce_kernel(sp, flt, piece, terms, total, held, arrived, sems):
+    group = Group(sp, flt)
+    greet_group(group)
+    start, middle, finish = sum_over_group(group, piece, terms, held, arrived, total, sems)
+    start()
+    middle()
+    finish()
+
+
+def reduced(term, cin, cout):
+    sp, flt = lax.axis_size("sp"), lax.axis_size("flt")
+    count = sp * flt
+    size = term.size // 256
+    piece = -(-size // (8 * count)) * 8
+    half = count * piece
+    packed = term.reshape(2, size, 128)
+    packed = jnp.pad(packed, ((0, 0), (0, half - size), (0, 0))).reshape(2 * half, 128)
+    out = pl.pallas_call(
+        functools.partial(reduce_kernel, sp, flt, piece),
+        out_shape=jax.ShapeDtypeStruct(packed.shape, jnp.float32),
+        in_specs=[pl.BlockSpec(memory_space=VMEM)],
+        out_specs=pl.BlockSpec(memory_space=VMEM),
+        scratch_shapes=[
+            VMEM((half, 128), jnp.float32),
+            VMEM((half, 128), jnp.float32),
+            pltpu.SemaphoreType.DMA((8, count)),
+        ],
+        compiler_params=pltpu.CompilerParams(collective_id=0, has_side_effects=True, vmem_limit_bytes=32 * 2**20),
+    )(packed)
+    return out.reshape(2, half, 128)[:, :size].reshape(term.shape)
 
 
 def padded_2(value, sides, width):
@@ -30,7 +210,7 @@
 
 
 def contract_last(left, right):
-    return lax.dot_general(left, right, (((1,), (1,)), ((), ())), precision=lax.Precision.HIGHEST)
+    return lax.dot_general(left, right, (((1,), (1,)), ((), ())), precision=lax.Precision.HIGH)
 
 
 def per_device(acts, grad_out, kernel):
@@ -56,14 +236,14 @@
             index = 3 * a_tap + b_tap
             slab = padded[:, 2 - a_tap, 2 - b_tap : 2 - b_tap + rows, :].reshape(cout, rows * width)
             partial_sum = partial_sum + jnp.dot(
-                weights_tap[index], slab, precision=lax.Precision.HIGHEST
+                weights_tap[index], slab, precision=lax.Precision.HIGH
             )
             weight_terms[index] = contract_last(source_stack, slab)
     parts_x = partial_sum.reshape(3, cin, rows, width)
     plane_out = take_next(parts_x[0]) + parts_x[1] + take_prior(parts_x[2])
     outputs = [plane_out]
     term = jnp.stack(weight_terms, axis=0).reshape(3, 3, 3, cin, cout) * factor
-    weight_grad = lax.psum(term, ("sp", "flt", "rep"))
+    weight_grad = reduced(term, cin, cout)
     input_grad = jnp.stack(outputs, axis=1)
     return (input_grad, weight_grad)
 

time: 148 us -> 60.9 us (0.41); the launches traced: 146 us -> 60.5 us
  waiting for transfers between devices: 93.2 us -> 10.4 us
  Pallas kernels: 0 us -> 18.8 us
  between operations: 14.4 us -> 1.1 us
  matrix products: 15 us -> 8.65 us
  local copies, waits for them, and re-layouts: 9.81 us -> 8.04 us
    psum x1 -> x0, waiting for transfers between devices: 82.7 us -> none  [per_device(): weight_grad = lax.psum(term, ('sp', 'flt', 'rep'))]
    pallas_call x0 -> x1, Pallas kernels: none -> 18.8 us  [reduced(): pl.pallas_call(functools.partial(reduce_kernel, sp, flt, piece), out_shap...]
    dot_general x9, matrix products: 7.91 us -> 4.59 us  [contract_last(): lax.dot_general(left, right, (((1,), (1,)), ((), ())), precision=lax.Prec...]
    dot_general x9, matrix products: 7.09 us -> 4.06 us  [per_device(): jnp.dot(weights_tap[index], slab, precision=lax.Precision.HIGH)]
    unnamed x24 -> x31, local copies, waits for them, and re-layouts: 5.03 us -> 2.83 us
  transfers between devices with their start and end apart: 5 -> 4, of which waited for: 5 -> 4; matrix products, arithmetic and copies ran while one was open for 7% -> 3% of each run, Pallas kernels for 0% -> 0%
where the time goes in v1:
time: 60.9 us; the launch traced here: 60.5 us
  Pallas kernels  18.8 us (31%)
  starting transfers between devices  12.3 us (20%)
  waiting for transfers between devices  10.4 us (17%)
  matrix products  8.65 us (14%)
  local copies, waits for them, and re-layouts  8.04 us (13%)
  other arithmetic  1.23 us (2%)
  between operations  1.1 us (2%)
    pallas_call x1, Pallas kernels, reduced(): pl.pallas_call(functools.partial(reduce_kernel, sp, flt, piece), out_shap...  18.8 us
    ppermute x2, starting transfers between devices, padded_2(): before = lax.ppermute(last, axis, up)  7.19 us
    ppermute x2, waiting for transfers between devices, padded_2(): after = lax.ppermute(first, axis, down)  5.61 us
    ppermute x2, starting transfers between devices, padded_2(): after = lax.ppermute(first, axis, down)  5.07 us
    ppermute x2, waiting for transfers between devices, padded_2(): before = lax.ppermute(last, axis, up)  4.82 us
    dot_general x9, matrix products, contract_last(): lax.dot_general(left, right, (((1,), (1,)), ((), ())), precision=lax.Prec...  4.59 us
    dot_general x9, matrix products, per_device(): jnp.dot(weights_tap[index], slab, precision=lax.Precision.HIGH)  4.06 us
    unnamed x31, local copies, waits for them, and re-layouts  2.83 us
  transfers between devices with their start and end apart: 4, of which 4 were waited for; matrix products, arithmetic and copies ran while one was open for 3% of the time, Pallas kernels for 0%

profile of v1, /device:TPU:1, one launch (start us, length us, event | category | flops | bytes accessed | tf_op | source)
XLA Modules:
  0.0 60.5 jit_solution(14479677961996569642)
XLA Ops:
  0.6 1.0 %copy.10 = f32[64,1,2,512]{3,0,2,1:T(8,128)S(1)} copy(f32[64,1,2,512]{3,2,1,0:T(2,128)} %param.4) | data formatting | bytes 524288 | tf_op args[1]
  1.6 4.2 %collective-permute-start = (f32[64,1,2,512]{3,0,2,1:T(8,128)S(1)}, f32[64,1,2,512]{3,0,2,1:T(8,128)S(1)}, u32[]{:S(2)}, u32[]{:S(2)}) collective-permute-start(f32[64,1,2,512]{3,0,2,1:T(8,128)S(1)} %copy.10), channel_id=1, source_target_pairs={{0,4},{4,8},{8,12},{1,5},{5,9},{9,13},{2,6},{6,10},{10,14},{3,7},{... | collective-permute-start | bytes 786440 | tf_op jit(solution)/shard_map/ppermute | solution.py:196
  5.8 1.3 %collective-permute-start.1 = (f32[64,1,2,512]{3,0,2,1:T(8,128)S(1)}, f32[64,1,2,512]{3,0,2,1:T(8,128)S(1)}, u32[]{:S(2)}, u32[]{:S(2)}) collective-permute-start(f32[64,1,2,512]{3,0,2,1:T(8,128)S(1)} %copy.10), channel_id=1, source_target_pairs={{4,0},{8,4},{12,8},{5,1},{9,5},{13,9},{6,2},{10,6},{14,10},{7,3},{... | collective-permute-start | bytes 786440 | tf_op jit(solution)/shard_map/ppermute | solution.py:197
  7.1 3.6 %collective-permute-done = f32[64,1,2,512]{3,0,2,1:T(8,128)S(1)} collective-permute-done((f32[64,1,2,512]{3,0,2,1:T(8,128)S(1)}, f32[64,1,2,512]{3,0,2,1:T(8,128)S(1)}, u32[]{:S(2)}, u32[]{:S(2)}) %collective-permute-start) | collective-permute-done | bytes 262176 | tf_op jit(solution)/shard_map/ppermute | solution.py:196
  10.9 3.7 %collective-permute-done.1 = f32[64,1,2,512]{3,0,2,1:T(8,128)S(1)} collective-permute-done((f32[64,1,2,512]{3,0,2,1:T(8,128)S(1)}, f32[64,1,2,512]{3,0,2,1:T(8,128)S(1)}, u32[]{:S(2)}, u32[]{:S(2)}) %collective-permute-start.1) | collective-permute-done | bytes 262176 | tf_op jit(solution)/shard_map/ppermute | solution.py:197
  14.7 3.8 %collective-permute-start.2 = (f32[64,3,1,512]{3,0,2,1:T(8,128)S(1)}, f32[64,3,1,512]{3,0,2,1:T(8,128)S(1)}, u32[]{:S(2)}, u32[]{:S(2)}) collective-permute-start(f32[64,3,1,512]{3,0,2,1:T(8,128)S(1)} %get-tuple-element.15), channel_id=1, source_target_pairs={{1,0},{2,1},{3,2},{5,4},{6,5},{7,6},{9,8},{10,9},{11,10},{13,12},{... | collective-permute-start | bytes 1179656 | tf_op jit(solution)/shard_map/ppermute | solution.py:197
  18.5 3.0 %collective-permute-start.3 = (f32[64,3,1,512]{3,0,2,1:T(8,128)S(1)}, f32[64,3,1,512]{3,0,2,1:T(8,128)S(1)}, u32[]{:S(2)}, u32[]{:S(2)}) collective-permute-start(f32[64,3,1,512]{3,0,2,1:T(8,128)S(1)} %get-tuple-element.14), channel_id=1, source_target_pairs={{0,1},{1,2},{2,3},{4,5},{5,6},{6,7},{8,9},{9,10},{10,11},{12,13},{... | collective-permute-start | bytes 1179656 | tf_op jit(solution)/shard_map/ppermute | solution.py:196
  21.5 0.3 fusion.16
  21.8 0.3 concatenate.41
  22.6 0.2 copy.14
  22.9 0.2 copy.19
  23.1 1.9 %collective-permute-done.2 = f32[64,3,1,512]{3,0,2,1:T(8,128)S(1)} collective-permute-done((f32[64,3,1,512]{3,0,2,1:T(8,128)S(1)}, f32[64,3,1,512]{3,0,2,1:T(8,128)S(1)}, u32[]{:S(2)}, u32[]{:S(2)}) %collective-permute-start.2) | collective-permute-done | bytes 393248 | tf_op jit(solution)/shard_map/ppermute | solution.py:197
  25.0 1.2 %collective-permute-done.3 = f32[64,3,1,512]{3,0,2,1:T(8,128)S(1)} collective-permute-done((f32[64,3,1,512]{3,0,2,1:T(8,128)S(1)}, f32[64,3,1,512]{3,0,2,1:T(8,128)S(1)}, u32[]{:S(2)}, u32[]{:S(2)}) %collective-permute-start.3) | collective-permute-done | bytes 393248 | tf_op jit(solution)/shard_map/ppermute | solution.py:196
  26.3 0.2 copy.13
  26.6 0.2 copy.15
  26.9 0.2 copy.16
  27.2 0.2 copy.17
  27.4 0.2 copy.18
  27.7 0.2 copy.20
  28.0 0.5 fusion.13
  28.5 0.5 fusion.12
  29.0 0.5 fusion.11
  29.5 0.5 fusion.10
  30.0 0.5 fusion.9
  30.5 0.5 fusion.8
  31.0 0.5 fusion.7
  31.6 0.5 fusion.6
  32.1 0.5 fusion.5
  32.6 0.3 copy.21
  32.9 0.2 mul.12
  33.2 18.8 %shard_map.50 = f32[896,128]{1,0:T(8,128)S(1)} custom-call(f32[896,128]{1,0:T(8,128)S(1)} %bitcast.161), custom_call_target="tpu_custom_call" | custom-call | tf_op jit(solution)/shard_map/pallas_call | solution.py:174
  52.0 1.1 %reshape.36 = f32[3,3,3,64,64]{4,3,2,1,0:T(8,128)} reshape(f32[2,432,128]{2,1,0:T(8,128)S(1)} %slice.127) | data formatting | bytes 884736 | tf_op jit(solution)/shard_map/reshape | solution.py:186
  53.3 0.5 convolution_bitcast_fusion.5
  53.8 0.4 convolution_add_fusion.2
  54.2 0.5 fusion.4
  54.7 0.5 copy-done.5
  55.2 0.4 fusion.3
  55.6 0.4 convolution_add_fusion.1
  56.1 0.5 fusion.2
  56.5 0.5 copy-done.3
  57.0 0.5 fusion.1
  57.5 0.4 convolution_add_fusion
  57.9 0.5 fusion
  58.5 0.2 squeeze.48
  58.7 0.3 slice.121
  59.0 0.2 squeeze.50
  59.3 0.2 squeeze.49
  59.5 1.0 %add_bitcast_fusion = f32[64,1,2,512]{3,2,1,0:T(2,128)} fusion(f32[64,2,511]{2,1,0:T(2,128)S(1)} %bitcast.197, f32[64,2,512]{2,1,0:T(2,128)S(1)} %squeeze.49, f32[64,2,511]{2,1,0:T(2,128)S(1)} %slice.121), kind=kLoop, calls=%fused_computation.39 | loop fusion | flops 131072 | bytes 1047552 | tf_op jit(solution)/shard_map/stack | solution.py:247
  (37 shorter events, 1.4 us)
Async XLA Ops:
  1.6 9.2 %copy-start.1 = (f32[64,1,2,512]{3,2,1,0:T(2,128)S(1)}, f32[64,1,2,512]{3,2,1,0:T(2,128)}, u32[]{:S(2)}) copy-start(f32[64,1,2,512]{3,2,1,0:T(2,128)} %param.4) | copy-start | bytes 786436
  1.6 9.1 %collective-permute-start = (f32[64,1,2,512]{3,0,2,1:T(8,128)S(1)}, f32[64,1,2,512]{3,0,2,1:T(8,128)S(1)}, u32[]{:S(2)}, u32[]{:S(2)}) collective-permute-start(f32[64,1,2,512]{3,0,2,1:T(8,128)S(1)} %copy.10), channel_id=1, source_target_pairs={{0,4},{4,8},{8,12},{1,5},{5,9},{9,13},{2,6},{6,10},{10,14},{3,7},{... | collective-permute-start | bytes 786440 | tf_op jit(solution)/shard_map/ppermute | solution.py:196
  5.8 8.8 %collective-permute-start.1 = (f32[64,1,2,512]{3,0,2,1:T(8,128)S(1)}, f32[64,1,2,512]{3,0,2,1:T(8,128)S(1)}, u32[]{:S(2)}, u32[]{:S(2)}) collective-permute-start(f32[64,1,2,512]{3,0,2,1:T(8,128)S(1)} %copy.10), channel_id=1, source_target_pairs={{4,0},{8,4},{12,8},{5,1},{9,5},{13,9},{6,2},{10,6},{14,10},{7,3},{... | collective-permute-start | bytes 786440 | tf_op jit(solution)/shard_map/ppermute | solution.py:197
  14.6 6.9 %copy-start = (f32[64,1,2,512]{3,2,1,0:T(2,128)S(1)}, f32[64,1,2,512]{3,2,1,0:T(2,128)}, u32[]{:S(2)}) copy-start(f32[64,1,2,512]{3,2,1,0:T(2,128)} %param.3) | copy-start | bytes 786436
  14.7 10.3 %collective-permute-start.2 = (f32[64,3,1,512]{3,0,2,1:T(8,128)S(1)}, f32[64,3,1,512]{3,0,2,1:T(8,128)S(1)}, u32[]{:S(2)}, u32[]{:S(2)}) collective-permute-start(f32[64,3,1,512]{3,0,2,1:T(8,128)S(1)} %get-tuple-element.15), channel_id=1, source_target_pairs={{1,0},{2,1},{3,2},{5,4},{6,5},{7,6},{9,8},{10,9},{11,10},{13,12},{... | collective-permute-start | bytes 1179656 | tf_op jit(solution)/shard_map/ppermute | solution.py:197
  18.5 7.7 %collective-permute-start.3 = (f32[64,3,1,512]{3,0,2,1:T(8,128)S(1)}, f32[64,3,1,512]{3,0,2,1:T(8,128)S(1)}, u32[]{:S(2)}, u32[]{:S(2)}) collective-permute-start(f32[64,3,1,512]{3,0,2,1:T(8,128)S(1)} %get-tuple-element.14), channel_id=1, source_target_pairs={{0,1},{1,2},{2,3},{4,5},{5,6},{6,7},{8,9},{9,10},{10,11},{12,13},{... | collective-permute-start | bytes 1179656 | tf_op jit(solution)/shard_map/ppermute | solution.py:196
  27.1 2.4 %copy-start.4 = (f32[8,8,2,512]{3,1,2,0:T(8,128)}, f32[8,8,2,512]{3,1,2,0:T(8,128)S(1)}, u32[]{:S(2)}) copy-start(f32[8,8,2,512]{3,1,2,0:T(8,128)S(1)} %copy.25) | copy-start | bytes 786436
  27.7 3.4 %copy-start.2 = (f32[8,8,2,512]{3,1,2,0:T(8,128)}, f32[8,8,2,512]{3,1,2,0:T(8,128)S(1)}, u32[]{:S(2)}) copy-start(f32[8,8,2,512]{3,1,2,0:T(8,128)S(1)} %copy.28) | copy-start | bytes 786436
  52.0 1.3 %copy-start.6 = (f32[3,3,3,64,64]{4,3,2,1,0:T(8,128)S(1)}, f32[3,3,3,64,64]{4,3,2,1,0:T(8,128)}, u32[]{:S(2)}) copy-start(f32[3,3,3,64,64]{4,3,2,1,0:T(8,128)} %param.5) | copy-start | bytes 1327108
  54.2 1.0 %copy-start.5 = (f32[8,8,2,512]{3,1,2,0:T(8,128)S(1)}, f32[8,8,2,512]{3,1,2,0:T(8,128)}, u32[]{:S(2)}) copy-start(f32[8,8,2,512]{3,1,2,0:T(8,128)} %copy-done.4) | copy-start | bytes 786436
  56.1 1.0 %copy-start.3 = (f32[8,8,2,512]{3,1,2,0:T(8,128)S(1)}, f32[8,8,2,512]{3,1,2,0:T(8,128)}, u32[]{:S(2)}) copy-start(f32[8,8,2,512]{3,1,2,0:T(8,128)} %copy-done.2) | copy-start | bytes 786436

commit v2 on v1

--- a/solution.py
+++ b/solution.py
@@ -134,118 +134,287 @@
     return start, middle, finish
 
 
-def greet(devices):
+def halves(value):
+    high = value.astype(jnp.bfloat16)
+    return high, (value - high.astype(jnp.float32)).astype(jnp.bfloat16)
+
+
+def moved(value, step):
+    width = value.shape[-1]
+    lane = lax.broadcasted_iota(jnp.int32, value.shape, 1)
+    edge = 0 if step == 1 else width - 1
+    return jnp.where(lane == edge, 0.0, pltpu.roll(value, step % width, 1))
+
+
+def product(left, right, dims):
+    (lh, ll), (rh, rl) = left, right
+
+    def dot(x, y):
+        return lax.dot_general(x, y, (dims, ((), ())), preferred_element_type=jnp.float32)
+
+    return dot(lh, rh) + dot(lh, rl) + dot(ll, rh)
+
+
+def backward_kernel(
+    sp, flt, piece, size, factor, acts, grad, weights, out, wgrad,
+    pad, high, low, acts_high, acts_low, w_high, w_low,
+    terms, held, arrived, total, send, recv, sems,
+):
+    group = Group(sp, flt)
+    core, count = group.core, group.count
+    z, x = lax.axis_index("sp"), lax.axis_index("flt")
+    cin, width = acts.shape[1:]
+    cout = grad.shape[1]
+    half = count * piece
+    z_exists = {0: z > 0, 2: z < sp - 1}
+    cross_x = x + 2 * core - 1
+    cross_exists = (cross_x >= 0) & (cross_x < flt)
+    cross = {"flt": cross_x, "rep": 1 - core}
+
     barrier = pltpu.get_barrier_semaphore()
-    for device in devices:
-        pl.semaphore_signal(barrier, 1, device_id=device, device_id_type=MESH)
-    return barrier
-
-
-def greet_group(group):
-    barrier = greet([group.partner()])
-
-    def run(k, carry):
+    pl.semaphore_signal(barrier, 1, device_id=group.partner(), device_id_type=MESH)
+
+    def signal(k, carry):
         pl.semaphore_signal(
             barrier, 1, device_id=group.peer(group.after(k)), device_id_type=MESH
         )
         return carry
 
-    lax.fori_loop(0, group.count - 1, run, 0)
-    pl.semaphore_wait(barrier, group.count)
-
-
-def reduce_kernel(sp, flt, piece, terms, total, held, arrived, sems):
-    group = Group(sp, flt)
-    greet_group(group)
+    lax.fori_loop(0, count - 1, signal, 0)
+
+    @pl.when(cross_exists)
+    def _():
+        pl.semaphore_signal(barrier, 1, device_id=cross, device_id_type=MESH)
+        pl.semaphore_wait(barrier, count + 1)
+
+    @pl.when(jnp.logical_not(cross_exists))
+    def _():
+        pl.semaphore_wait(barrier, count)
+
+    def copy(src, index, slot, device):
+        return pltpu.make_async_remote_copy(
+            src, pad.at[index], send.at[slot], recv.at[index],
+            device_id=device, device_id_type=MESH,
+        )
+
+    def to_z(plane, row):
+        return copy(grad.at[row], (2 - plane) * 4 + 1 + row, plane + row, {"sp": z + plane - 1})
+
+    def edge(plane, row):
+        return grad.at[row - 1] if plane == 1 else pad.at[plane * 4 + row]
+
+    def to_cross(plane):
+        return copy(edge(plane, 1 + core), plane * 4 + 3 * (1 - core), 4 + plane, cross)
+
+    def to_partner(plane):
+        return copy(edge(plane, 2 - core), plane * 4 + 3 * core, 7 + plane, group.partner())
+
+    def await_row(plane, row):
+        index = plane * 4 + row
+        copy(grad.at[0], index, 0, group.partner()).wait_recv()
+
+    for plane in (0, 2):
+
+        @pl.when(z_exists[plane])
+        def _():
+            to_z(plane, core).start()
+
+    @pl.when(cross_exists)
+    def _():
+        to_cross(1).start()
+
+    to_partner(1).start()
+    for plane in (0, 2):
+
+        @pl.when(z_exists[plane])
+        def _():
+            to_z(plane, 1 - core).start()
+
+    def keep(plane, row, value):
+        at = pl.ds(pl.multiple_of(row * cout, cout), cout)
+        high[plane, at, :], low[plane, at, :] = halves(value)
+
+    for row in range(2):
+        keep(1, 1 + row, grad[row])
+        line = acts[row]
+        for c, value in enumerate((moved(line, 1), line, moved(line, -1))):
+            at = pl.ds(c * cin, cin)
+            acts_high[row, at, :], acts_low[row, at, :] = halves(value)
+    for a in range(3):
+        for c in range(3):
+            taps = jnp.concatenate([weights[9 * a + 3 * b + c] for b in (2, 1, 0)], axis=1)
+            at = pl.ds(c * cin, cin)
+            w_high[a, at, :], w_low[a, at, :] = halves(taps)
+
+    def place(row):
+        return row if row < size else row - size + half
+
+    def put(row, value):
+        rows = value.shape[0]
+        first = min(max(size - row, 0), rows)
+        if first:
+            terms[pl.ds(row, first), :] = value[:first]
+        if rows - first:
+            terms[pl.ds(place(row + first), rows - first), :] = value[first:]
+
+    if half > size:
+        for owner in range(2):
+            terms[pl.ds(owner * half + size, half - size), :] = jnp.zeros(
+                (half - size, 128), jnp.float32
+            )
+
+    blocks = 3 * cout
+    each_tap = 9 * cin * cout // 128
+
+    def weight_terms(a):
+        plane = 2 - a
+        result = jnp.zeros((3 * cin, blocks), jnp.float32)
+        for row in range(2):
+            at = pl.ds(row * cout, blocks)
+            result = result + product(
+                (acts_high[row], acts_low[row]),
+                (high[plane, at, :], low[plane, at, :]),
+                ((1,), (1,)),
+            )
+        put(a * each_tap, result[:, :128])
+        rest = result[:, 128:]
+        middle = 3 * cin // 2
+        put(a * each_tap + 3 * cin, jnp.concatenate([rest[:middle], rest[middle:]], axis=1))
+
+    def take(plane, row, exists):
+        @pl.when(exists)
+        def _():
+            await_row(plane, row)
+            keep(plane, row, pad[plane * 4 + row])
+
+        @pl.when(jnp.logical_not(exists))
+        def _():
+            keep(plane, row, jnp.zeros((cout, width), jnp.float32))
+
+    always = z >= 0
+    for plane in (0, 2):
+
+        @pl.when(z_exists[plane])
+        def _():
+            await_row(plane, 1 + core)
+
+            @pl.when(cross_exists)
+            def _():
+                to_cross(plane).start()
+
+    take(1, 3 * (1 - core), always)
+    take(1, 3 * core, cross_exists)
+    weight_terms(1)
+    for plane in (0, 2):
+
+        @pl.when(z_exists[plane])
+        def _():
+            await_row(plane, 2 - core)
+            to_partner(plane).start()
+            keep(plane, 1, pad[plane * 4 + 1])
+            keep(plane, 2, pad[plane * 4 + 2])
+
+        @pl.when(jnp.logical_not(z_exists[plane]))
+        def _():
+            for row in (1, 2):
+                keep(plane, row, jnp.zeros((cout, width), jnp.float32))
+
+    for plane in (0, 2):
+        take(plane, 3 * (1 - core), z_exists[plane])
+        take(plane, 3 * core, z_exists[plane] & cross_exists)
+        weight_terms(2 - plane)
+
     start, middle, finish = sum_over_group(group, piece, terms, held, arrived, total, sems)
     start()
     middle()
+    for row in range(2):
+        at = pl.ds(row * cout, blocks)
+        result = jnp.zeros((3 * cin, width), jnp.float32)
+        for a in range(3):
+            result = result + product(
+                (w_high[a], w_low[a]), (high[2 - a, at, :], low[2 - a, at, :]), ((1,), (0,))
+            )
+        out[row] = (
+            moved(result[:cin], -1) + result[cin : 2 * cin] + moved(result[2 * cin :], 1)
+        )
+    for plane in (0, 2):
+
+        @pl.when(z_exists[plane])
+        def _():
+            to_z(plane, core).wait_send()
+            to_z(plane, 1 - core).wait_send()
+            to_partner(plane).wait_send()
+
+        @pl.when(z_exists[plane] & cross_exists)
+        def _():
+            to_cross(plane).wait_send()
+
+    to_partner(1).wait_send()
+
+    @pl.when(cross_exists)
+    def _():
+        to_cross(1).wait_send()
+
     finish()
-
-
-def reduced(term, cin, cout):
+    step = 16
+    for a in range(3):
+        for c in range(3):
+            for i in range(0, cin, step):
+                line = c * cin + i
+                both = total[pl.ds(place(a * each_tap + line), step), :] * factor
+                wrapped, lane = line % (3 * cin // 2), line // (3 * cin // 2) * cout
+                last = total[pl.ds(place(a * each_tap + 3 * cin + wrapped), step), :] * factor
+                at = pl.ds(i, step)
+                wgrad[9 * a + 6 + c, at, :] = both[:, :cout]
+                wgrad[9 * a + 3 + c, at, :] = both[:, cout:]
+                wgrad[9 * a + c, at, :] = last[:, lane : lane + cout]
+
+
+def per_device(acts, grad_out, kernel):
+    cin, planes, rows, width = acts.shape
+    cout = grad_out.shape[0]
     sp, flt = lax.axis_size("sp"), lax.axis_size("flt")
     count = sp * flt
-    size = term.size // 256
+    voxels = planes * sp * rows * flt * lax.axis_size("rep") * width
+    factor = 1.0 / math.sqrt(voxels)
+    size = kernel.size // 256
     piece = -(-size // (8 * count)) * 8
     half = count * piece
-    packed = term.reshape(2, size, 128)
-    packed = jnp.pad(packed, ((0, 0), (0, half - size), (0, 0))).reshape(2 * half, 128)
-    out = pl.pallas_call(
-        functools.partial(reduce_kernel, sp, flt, piece),
-        out_shape=jax.ShapeDtypeStruct(packed.shape, jnp.float32),
-        in_specs=[pl.BlockSpec(memory_space=VMEM)],
-        out_specs=pl.BlockSpec(memory_space=VMEM),
+    f32, bf16 = jnp.float32, jnp.bfloat16
+    vmem = pl.BlockSpec(memory_space=VMEM)
+    out, wgrad = pl.pallas_call(
+        functools.partial(backward_kernel, sp, flt, piece, size, factor),
+        out_shape=(
+            jax.ShapeDtypeStruct((rows, cin, width), f32),
+            jax.ShapeDtypeStruct((27, cin, cout), f32),
+        ),
+        in_specs=[vmem] * 3,
+        out_specs=(vmem, vmem),
         scratch_shapes=[
-            VMEM((half, 128), jnp.float32),
-            VMEM((half, 128), jnp.float32),
+            VMEM((12, cout, width), f32),
+            VMEM((3, 4 * cout, width), bf16),
+            VMEM((3, 4 * cout, width), bf16),
+            VMEM((2, 3 * cin, width), bf16),
+            VMEM((2, 3 * cin, width), bf16),
+            VMEM((3, 3 * cin, 3 * cout), bf16),
+            VMEM((3, 3 * cin, 3 * cout), bf16),
+            VMEM((2 * half, 128), f32),
+            VMEM((half, 128), f32),
+            VMEM((half, 128), f32),
+            VMEM((2 * half, 128), f32),
+            pltpu.SemaphoreType.DMA((10,)),
+            pltpu.SemaphoreType.DMA((12,)),
             pltpu.SemaphoreType.DMA((8, count)),
         ],
-        compiler_params=pltpu.CompilerParams(collective_id=0, has_side_effects=True, vmem_limit_bytes=32 * 2**20),
-    )(packed)
-    return out.reshape(2, half, 128)[:, :size].reshape(term.shape)
-
-
-def padded_2(value, sides, width):
-    for axis, dim in sides:
-        count, length = (lax.axis_size(axis), value.shape[dim])
-        up = [(i, (i + 1) % count) for i in range(count - 1)]
-        down = [(j, i) for i, j in up]
-        last = lax.slice_in_dim(value, length - width, length, axis=dim)
-        first = lax.slice_in_dim(value, 0, width, axis=dim)
-        before = lax.ppermute(last, axis, up)
-        after = lax.ppermute(first, axis, down)
-        value = jnp.concatenate([before, value, after], axis=dim)
-    return value
-
-
-def take_next(values):
-    edge = jnp.zeros(values.shape[:-1] + (1,), values.dtype)
-    return jnp.concatenate([values[..., 1:], edge], axis=-1)
-
-
-def take_prior(values):
-    edge = jnp.zeros(values.shape[:-1] + (1,), values.dtype)
-    return jnp.concatenate([edge, values[..., :-1]], axis=-1)
-
-
-def contract_last(left, right):
-    return lax.dot_general(left, right, (((1,), (1,)), ((), ())), precision=lax.Precision.HIGH)
-
-
-def per_device(acts, grad_out, kernel):
-    cin = acts.shape[0]
-    planes = acts.shape[1]
-    rows = acts.shape[2]
-    width = acts.shape[3]
-    cout = grad_out.shape[0]
-    voxels = (
-        planes * lax.axis_size("sp") * rows * lax.axis_size("flt") * lax.axis_size("rep") * width
+        compiler_params=pltpu.CompilerParams(
+            collective_id=0, has_side_effects=True, vmem_limit_bytes=40 * 2**20
+        ),
+    )(
+        acts[:, 0].transpose(1, 0, 2),
+        grad_out[:, 0].transpose(1, 0, 2),
+        kernel.reshape(27, cin, cout),
     )
-    factor = 1.0 / math.sqrt(voxels)
-    padded = padded_2(grad_out, (("sp", 1), (("flt", "rep"), 2)), 1)
-    weights_tap = kernel.reshape(9, 3 * cin, cout)
-    weight_terms = [jnp.zeros((3 * cin, cout), jnp.float32) for index in range(9)]
-    source = acts[:, 0]
-    source_stack = jnp.concatenate([take_prior(source), source, take_next(source)], axis=0).reshape(
-        3 * cin, rows * width
-    )
-    partial_sum = jnp.zeros((3 * cin, rows * width), jnp.float32)
-    for a_tap in range(3):
-        for b_tap in range(3):
-            index = 3 * a_tap + b_tap
-            slab = padded[:, 2 - a_tap, 2 - b_tap : 2 - b_tap + rows, :].reshape(cout, rows * width)
-            partial_sum = partial_sum + jnp.dot(
-                weights_tap[index], slab, precision=lax.Precision.HIGH
-            )
-            weight_terms[index] = contract_last(source_stack, slab)
-    parts_x = partial_sum.reshape(3, cin, rows, width)
-    plane_out = take_next(parts_x[0]) + parts_x[1] + take_prior(parts_x[2])
-    outputs = [plane_out]
-    term = jnp.stack(weight_terms, axis=0).reshape(3, 3, 3, cin, cout) * factor
-    weight_grad = reduced(term, cin, cout)
-    input_grad = jnp.stack(outputs, axis=1)
-    return (input_grad, weight_grad)
+    return out.transpose(1, 0, 2)[:, None], wgrad.reshape(kernel.shape)
 
 
 def solution(mesh):

time: 60.9 us -> 35 us (0.57)
  Pallas kernels: 18.8 us -> 31.1 us
  starting transfers between devices: 12.3 us -> 0 us
  waiting for transfers between devices: 10.4 us -> 0 us
  matrix products: 8.65 us -> 0 us
  local copies, waits for them, and re-layouts: 8.04 us -> 3.13 us
  other arithmetic: 1.23 us -> 0 us
    ppermute x4 -> x0, starting transfers between devices: 12.3 us -> none  [the longest x2 7.19 us: padded_2(): before = lax.ppermute(last, axis, up)]
    pallas_call x1, Pallas kernels: 18.8 us -> 31.1 us  [per_device(): pl.pallas_call(functools.partial(backward_kernel, sp, flt, piece, size, f...]
    ppermute x4 -> x0, waiting for transfers between devices: 10.4 us -> none  [the longest x2 5.61 us: padded_2(): after = lax.ppermute(first, axis, down)]
    dot_general x18 -> x0, matrix products: 8.65 us -> none  [the longest x9 4.59 us: contract_last(): lax.dot_general(left, right, (((1,), (1,)), ((), ())), precision=lax.Prec...]
    slice x11 -> x0, local copies, waits for them, and re-layouts: 2.05 us -> none  [the longest x6 1.23 us: per_device(): padded[:, 2 - a_tap, 2 - b_tap:2 - b_tap + rows, :]]
    transpose x0 -> x1, local copies, waits for them, and re-layouts: none -> 1.21 us  [per_device(): grad_out[:, 0].transpose(1, 0, 2)]
    reshape x1 -> x0, local copies, waits for them, and re-layouts: 1.12 us -> none  [reduced(): return out.reshape(2, half, 128)[:, :size].reshape(term.shape)]
    another operation x1 -> x0, other arithmetic: 1.04 us -> none  [per_device(): input_grad = jnp.stack(outputs, axis=1)]
  transfers between devices with their start and end apart: 4 -> 0, of which waited for: 4 -> 0; matrix products, arithmetic and copies ran while one was open for 3% -> 0% of each run, Pallas kernels for 0% -> 0%
where the time goes in v2:
time: 35 us; the launch traced here: 34.8 us
  Pallas kernels  31.1 us (89%)
  local copies, waits for them, and re-layouts  3.13 us (9%)
  between operations  0.65 us (2%)
    pallas_call x1, Pallas kernels, per_device(): pl.pallas_call(functools.partial(backward_kernel, sp, flt, piece, size, f...  31.1 us
    unnamed x4, local copies, waits for them, and re-layouts  1.92 us
    transpose x1, local copies, waits for them, and re-layouts, per_device(): grad_out[:, 0].transpose(1, 0, 2)  1.21 us

profile of v2, /device:TPU:1, one launch (start us, length us, event | category | flops | bytes accessed | tf_op | source)
XLA Modules:
  0.0 34.8 jit_solution(4451446704011361795)
XLA Ops:
  0.6 0.0 copy-start
  0.6 1.2 %copy_bitcast_fusion = (f32[2,64,512]{2,1,0:T(8,128)S(1)}, f32[2,64,512]{2,1,0:T(8,128)S(1)}) fusion(f32[64,1,2,512]{3,2,1,0:T(2,128)} %param.4, f32[64,1,2,512]{3,2,1,0:T(2,128)} %param.3), kind=kLoop, calls=%fused_computation | loop fusion | bytes 1048576 | tf_op jit(solution)/shard_map/transpose | solution.py:414
  1.9 0.1 copy-done
  2.0 31.1 %shard_map.50 = (f32[2,64,512]{2,1,0:T(8,128)S(1)}, f32[27,64,64]{2,1,0:T(8,128)S(1)}) custom-call(f32[2,64,512]{2,1,0:T(8,128)S(1)} %get-tuple-element.9.acts, f32[2,64,512]{2,1,0:T(8,128)S(1)} %get-tuple-element.8.grad, f32[27,64,64]{2,1,0:T(8,128)S(1)} %bitcast.14), custom_call_target="tpu_custom_call" | custom-call | tf_op jit(solution)/shard_map/pallas_call | solution.py:385
  33.0 0.9 %copy.7 = f32[64,1,2,512]{3,2,1,0:T(2,128)} copy(f32[64,1,2,512]{3,0,2,1:T(8,128)S(1)} %bitcast.15) | data formatting | bytes 524288
  33.9 0.9 %copy.11 = f32[3,3,3,64,64]{4,3,2,1,0:T(8,128)} copy(f32[3,3,3,64,64]{4,3,2,1,0:T(8,128)S(1)} %bitcast.13) | data formatting | bytes 884736
Async XLA Ops:
  0.6 1.3 %copy-start = (f32[3,3,3,64,64]{4,3,2,1,0:T(8,128)S(1)}, f32[3,3,3,64,64]{4,3,2,1,0:T(8,128)}, u32[]{:S(2)}) copy-start(f32[3,3,3,64,64]{4,3,2,1,0:T(8,128)} %param.5) | copy-start | bytes 1327108

commit v3 on v2

--- a/solution.py
+++ b/solution.py
@@ -114,11 +114,13 @@
         gather(j, j).wait_recv()
         pass_on(j, core).start()
 
-    def finish():
+    def reduce():
         each(count - 1, add_arrived)
         total[rows(core * half + chip * piece), :] = held[rows(chip * piece), :]
         each(count - 1, lambda k: gather(group.after(k), chip).start())
         pass_on(chip, core).start()
+
+    def finish():
         each(count - 1, forward)
         each(count, lambda k: pass_on(k, 1 - core).wait_recv())
         each(count, lambda k: to_partner(k).wait_send())
@@ -131,7 +133,7 @@
 
         each(count - 1, sent)
 
-    return start, middle, finish
+    return start, middle, reduce, finish
 
 
 def halves(value):
@@ -156,16 +158,17 @@
 
 
 def backward_kernel(
-    sp, flt, piece, size, factor, acts, grad, weights, out, wgrad,
+    sp, flt, pieces, sizes, factor, acts, grad, weights, out, wgrad,
     pad, high, low, acts_high, acts_low, w_high, w_low,
-    terms, held, arrived, total, send, recv, sems,
+    send, recv, *buffers,
 ):
+    buffers = (buffers[:5], buffers[5:])
     group = Group(sp, flt)
     core, count = group.core, group.count
     z, x = lax.axis_index("sp"), lax.axis_index("flt")
     cin, width = acts.shape[1:]
     cout = grad.shape[1]
-    half = count * piece
+    halves_of = [count * piece for piece in pieces]
     z_exists = {0: z > 0, 2: z < sp - 1}
     cross_x = x + 2 * core - 1
     cross_exists = (cross_x >= 0) & (cross_x < flt)
@@ -246,25 +249,27 @@
             at = pl.ds(c * cin, cin)
             w_high[a, at, :], w_low[a, at, :] = halves(taps)
 
-    def place(row):
-        return row if row < size else row - size + half
-
-    def put(row, value):
-        rows = value.shape[0]
-        first = min(max(size - row, 0), rows)
+    def place(chunk, row):
+        size = sizes[chunk]
+        return row if row < size else row - size + halves_of[chunk]
+
+    def put(chunk, row, value):
+        terms, rows = buffers[chunk][0], value.shape[0]
+        first = min(max(sizes[chunk] - row, 0), rows)
         if first:
             terms[pl.ds(row, first), :] = value[:first]
         if rows - first:
-            terms[pl.ds(place(row + first), rows - first), :] = value[first:]
-
-    if half > size:
-        for owner in range(2):
-            terms[pl.ds(owner * half + size, half - size), :] = jnp.zeros(
-                (half - size, 128), jnp.float32
-            )
+            terms[pl.ds(place(chunk, row + first), rows - first), :] = value[first:]
+
+    for chunk in range(2):
+        spare = halves_of[chunk] - sizes[chunk]
+        for owner in range(2 if spare else 0):
+            at = pl.ds(owner * halves_of[chunk] + sizes[chunk], spare)
+            buffers[chunk][0][at, :] = jnp.zeros((spare, 128), jnp.float32)
 
     blocks = 3 * cout
     each_tap = 9 * cin * cout // 128
+    base = ((1, each_tap), (0, 0), (1, 0))
 
     def weight_terms(a):
         plane = 2 - a
@@ -276,10 +281,11 @@
                 (high[plane, at, :], low[plane, at, :]),
                 ((1,), (1,)),
             )
-        put(a * each_tap, result[:, :128])
+        chunk, at = base[a]
+        put(chunk, at, result[:, :128])
         rest = result[:, 128:]
         middle = 3 * cin // 2
-        put(a * each_tap + 3 * cin, jnp.concatenate([rest[:middle], rest[middle:]], axis=1))
+        put(chunk, at + 3 * cin, jnp.concatenate([rest[:middle], rest[middle:]], axis=1))
 
     def take(plane, row, exists):
         @pl.when(exists)
@@ -305,6 +311,10 @@
     take(1, 3 * (1 - core), always)
     take(1, 3 * core, cross_exists)
     weight_terms(1)
+    sums = [
+        sum_over_group(group, pieces[i], *buffers[i]) for i in range(2)
+    ]
+    sums[0][0]()
     for plane in (0, 2):
 
         @pl.when(z_exists[plane])
@@ -319,14 +329,15 @@
             for row in (1, 2):
                 keep(plane, row, jnp.zeros((cout, width), jnp.float32))
 
+    sums[0][1]()
     for plane in (0, 2):
         take(plane, 3 * (1 - core), z_exists[plane])
         take(plane, 3 * core, z_exists[plane] & cross_exists)
         weight_terms(2 - plane)
 
-    start, middle, finish = sum_over_group(group, piece, terms, held, arrived, total, sems)
-    start()
-    middle()
+    sums[1][0]()
+    sums[0][2]()
+    sums[1][1]()
     for row in range(2):
         at = pl.ds(row * cout, blocks)
         result = jnp.zeros((3 * cin, width), jnp.float32)
@@ -337,6 +348,7 @@
         out[row] = (
             moved(result[:cin], -1) + result[cin : 2 * cin] + moved(result[2 * cin :], 1)
         )
+    sums[1][2]()
     for plane in (0, 2):
 
         @pl.when(z_exists[plane])
@@ -355,15 +367,18 @@
     def _():
         to_cross(1).wait_send()
 
-    finish()
+    sums[0][3]()
+    sums[1][3]()
     step = 16
     for a in range(3):
         for c in range(3):
             for i in range(0, cin, step):
                 line = c * cin + i
-                both = total[pl.ds(place(a * each_tap + line), step), :] * factor
+                chunk, first = base[a]
+                total = buffers[chunk][3]
+                both = total[pl.ds(place(chunk, first + line), step), :] * factor
                 wrapped, lane = line % (3 * cin // 2), line // (3 * cin // 2) * cout
-                last = total[pl.ds(place(a * each_tap + 3 * cin + wrapped), step), :] * factor
+                last = total[pl.ds(place(chunk, first + 3 * cin + wrapped), step), :] * factor
                 at = pl.ds(i, step)
                 wgrad[9 * a + 6 + c, at, :] = both[:, :cout]
                 wgrad[9 * a + 3 + c, at, :] = both[:, cout:]
@@ -377,13 +392,12 @@
     count = sp * flt
     voxels = planes * sp * rows * flt * lax.axis_size("rep") * width
     factor = 1.0 / math.sqrt(voxels)
-    size = kernel.size // 256
-    piece = -(-size // (8 * count)) * 8
-    half = count * piece
+    sizes = (kernel.size // 256 // 3, kernel.size // 256 * 2 // 3)
+    pieces = tuple(-(-size // (8 * count)) * 8 for size in sizes)
     f32, bf16 = jnp.float32, jnp.bfloat16
     vmem = pl.BlockSpec(memory_space=VMEM)
     out, wgrad = pl.pallas_call(
-        functools.partial(backward_kernel, sp, flt, piece, size, factor),
+        functools.partial(backward_kernel, sp, flt, pieces, sizes, factor),
         out_shape=(
             jax.ShapeDtypeStruct((rows, cin, width), f32),
             jax.ShapeDtypeStruct((27, cin, cout), f32),
@@ -398,13 +412,18 @@
             VMEM((2, 3 * cin, width), bf16),
             VMEM((3, 3 * cin, 3 * cout), bf16),
             VMEM((3, 3 * cin, 3 * cout), bf16),
-            VMEM((2 * half, 128), f32),
-            VMEM((half, 128), f32),
-            VMEM((half, 128), f32),
-            VMEM((2 * half, 128), f32),
             pltpu.SemaphoreType.DMA((10,)),
             pltpu.SemaphoreType.DMA((12,)),
-            pltpu.SemaphoreType.DMA((8, count)),
+        ] + [
+            kind
+            for piece in pieces
+            for kind in (
+                VMEM((2 * count * piece, 128), f32),
+                VMEM((count * piece, 128), f32),
+                VMEM((count * piece, 128), f32),
+                VMEM((2 * count * piece, 128), f32),
+                pltpu.SemaphoreType.DMA((8, count)),
+            )
         ],
         compiler_params=pltpu.CompilerParams(
             collective_id=0, has_side_effects=True, vmem_limit_bytes=40 * 2**20

time: 35 us -> 36.4 us (1.040)
  Pallas kernels: 31.1 us -> 32.5 us
    pallas_call x1, Pallas kernels: 31.1 us -> 32.5 us  [per_device(): pl.pallas_call(functools.partial(backward_kernel, sp, flt, pieces, sizes,...]
where the time goes in v3:
time: 36.4 us; the launch traced here: 36.3 us
  Pallas kernels  32.5 us (89%)
  local copies, waits for them, and re-layouts  3.13 us (9%)
  between operations  0.65 us (2%)
    pallas_call x1, Pallas kernels, per_device(): pl.pallas_call(functools.partial(backward_kernel, sp, flt, pieces, sizes,...  32.5 us
    unnamed x4, local copies, waits for them, and re-layouts  1.92 us
    transpose x1, local copies, waits for them, and re-layouts, per_device(): grad_out[:, 0].transpose(1, 0, 2)  1.21 us

profile of v3, /device:TPU:1, one launch (start us, length us, event | category | flops | bytes accessed | tf_op | source)
XLA Modules:
  0.0 36.3 jit_solution(11797175279693851835)
XLA Ops:
  0.6 0.0 copy-start
  0.6 1.2 %copy_bitcast_fusion = (f32[2,64,512]{2,1,0:T(8,128)S(1)}, f32[2,64,512]{2,1,0:T(8,128)S(1)}) fusion(f32[64,1,2,512]{3,2,1,0:T(2,128)} %param.4, f32[64,1,2,512]{3,2,1,0:T(2,128)} %param.3), kind=kLoop, calls=%fused_computation | loop fusion | bytes 1048576 | tf_op jit(solution)/shard_map/transpose | solution.py:433
  1.9 0.1 copy-done
  2.0 32.5 %shard_map.50 = (f32[2,64,512]{2,1,0:T(8,128)S(1)}, f32[27,64,64]{2,1,0:T(8,128)S(1)}) custom-call(f32[2,64,512]{2,1,0:T(8,128)S(1)} %get-tuple-element.9.acts, f32[2,64,512]{2,1,0:T(8,128)S(1)} %get-tuple-element.8.grad, f32[27,64,64]{2,1,0:T(8,128)S(1)} %bitcast.14), custom_call_target="tpu_custom_call" | custom-call | tf_op jit(solution)/shard_map/pallas_call | solution.py:399
  34.5 0.9 %copy.7 = f32[64,1,2,512]{3,2,1,0:T(2,128)} copy(f32[64,1,2,512]{3,0,2,1:T(8,128)S(1)} %bitcast.15) | data formatting | bytes 524288
  35.4 0.9 %copy.11 = f32[3,3,3,64,64]{4,3,2,1,0:T(8,128)} copy(f32[3,3,3,64,64]{4,3,2,1,0:T(8,128)S(1)} %bitcast.13) | data formatting | bytes 884736
Async XLA Ops:
  0.6 1.3 %copy-start = (f32[3,3,3,64,64]{4,3,2,1,0:T(8,128)S(1)}, f32[3,3,3,64,64]{4,3,2,1,0:T(8,128)}, u32[]{:S(2)}) copy-start(f32[3,3,3,64,64]{4,3,2,1,0:T(8,128)} %param.5) | copy-start | bytes 1327108

commit v4 on v2

--- a/solution.py
+++ b/solution.py
@@ -31,7 +31,7 @@
         return lax.rem(self.chip + 2 * self.count - 1 - step, self.count)
 
 
-def sum_over_group(group, piece, terms, held, arrived, total, sems):
+def sum_over_group(group, piece, share, terms, held, arrived, total, sems):
     core, chip, count = group.core, group.chip, group.count
     half = count * piece
 
@@ -40,8 +40,8 @@
 
     def to_partner(j):
         return pltpu.make_async_remote_copy(
-            terms.at[rows((1 - core) * half + j * piece)],
-            held.at[rows(j * piece)],
+            terms.at[pl.ds(pl.multiple_of((1 - core) * half + j * share, 8), share)],
+            held.at[pl.ds(j * share, share)],
             sems.at[0, j],
             sems.at[1, j],
             device_id=group.partner(),
@@ -87,12 +87,11 @@
 
         lax.fori_loop(0, steps, run, 0)
 
-    def start():
-        each(count, lambda k: to_partner(group.after(k)).start())
+    def start(a):
+        to_partner(a).start()
 
     def add_and_scatter(k):
         j = group.after(k)
-        to_partner(j).wait_recv()
         own = rows(j * piece)
         held[own, :] = held[own, :] + terms[rows(core * half + j * piece), :]
 
@@ -107,6 +106,8 @@
         held[own, :] = held[own, :] + arrived[rows(j * piece), :]
 
     def middle():
+        for a in range(3):
+            to_partner(a).wait_recv()
         each(count, add_and_scatter)
 
     def forward(k):
@@ -121,7 +122,8 @@
         pass_on(chip, core).start()
         each(count - 1, forward)
         each(count, lambda k: pass_on(k, 1 - core).wait_recv())
-        each(count, lambda k: to_partner(k).wait_send())
+        for a in range(3):
+            to_partner(a).wait_send()
         each(count, lambda k: pass_on(k, core).wait_send())
 
         def sent(k):
@@ -246,25 +248,29 @@
             at = pl.ds(c * cin, cin)
             w_high[a, at, :], w_low[a, at, :] = halves(taps)
 
-    def place(row):
-        return row if row < size else row - size + half
-
-    def put(row, value):
+    share = size // 3
+
+    def place(a, row):
+        return row // share * half + a * share + row % share
+
+    def put(a, row, value):
         rows = value.shape[0]
-        first = min(max(size - row, 0), rows)
+        first = min(max(share - row, 0), rows)
         if first:
-            terms[pl.ds(row, first), :] = value[:first]
+            terms[pl.ds(place(a, row), first), :] = value[:first]
         if rows - first:
-            terms[pl.ds(place(row + first), rows - first), :] = value[first:]
+            terms[pl.ds(place(a, row + first), rows - first), :] = value[first:]
 
     if half > size:
+        spare = jnp.zeros((half - size, 128), jnp.float32)
+        held[pl.ds(size, half - size), :] = spare
         for owner in range(2):
-            terms[pl.ds(owner * half + size, half - size), :] = jnp.zeros(
-                (half - size, 128), jnp.float32
-            )
-
+            terms[pl.ds(owner * half + size, half - size), :] = spare
+
+    start, middle, finish = sum_over_group(
+        group, piece, share, terms, held, arrived, total, sems
+    )
     blocks = 3 * cout
-    each_tap = 9 * cin * cout // 128
 
     def weight_terms(a):
         plane = 2 - a
@@ -276,10 +282,11 @@
                 (high[plane, at, :], low[plane, at, :]),
                 ((1,), (1,)),
             )
-        put(a * each_tap, result[:, :128])
+        put(a, 0, result[:, :128])
         rest = result[:, 128:]
-        middle = 3 * cin // 2
-        put(a * each_tap + 3 * cin, jnp.concatenate([rest[:middle], rest[middle:]], axis=1))
+        split = 3 * cin // 2
+        put(a, 3 * cin, jnp.concatenate([rest[:split], rest[split:]], axis=1))
+        start(a)
 
     def take(plane, row, exists):
         @pl.when(exists)
@@ -324,8 +331,6 @@
         take(plane, 3 * core, z_exists[plane] & cross_exists)
         weight_terms(2 - plane)
 
-    start, middle, finish = sum_over_group(group, piece, terms, held, arrived, total, sems)
-    start()
     middle()
     for row in range(2):
         at = pl.ds(row * cout, blocks)
@@ -361,9 +366,9 @@
         for c in range(3):
             for i in range(0, cin, step):
                 line = c * cin + i
-                both = total[pl.ds(place(a * each_tap + line), step), :] * factor
+                both = total[pl.ds(place(a, line), step), :] * factor
                 wrapped, lane = line % (3 * cin // 2), line // (3 * cin // 2) * cout
-                last = total[pl.ds(place(a * each_tap + 3 * cin + wrapped), step), :] * factor
+                last = total[pl.ds(place(a, 3 * cin + wrapped), step), :] * factor
                 at = pl.ds(i, step)
                 wgrad[9 * a + 6 + c, at, :] = both[:, :cout]
                 wgrad[9 * a + 3 + c, at, :] = both[:, cout:]
@@ -404,7 +409,7 @@
             VMEM((2 * half, 128), f32),
             pltpu.SemaphoreType.DMA((10,)),
             pltpu.SemaphoreType.DMA((12,)),
-            pltpu.SemaphoreType.DMA((8, count)),
+            pltpu.SemaphoreType.DMA((8, max(count, 3))),
         ],
         compiler_params=pltpu.CompilerParams(
             collective_id=0, has_side_effects=True, vmem_limit_bytes=40 * 2**20

time: 35 us -> 36.1 us (1.031)
  Pallas kernels: 31.1 us -> 32.2 us
    pallas_call x1, Pallas kernels: 31.1 us -> 32.2 us  [per_device(): pl.pallas_call(functools.partial(backward_kernel, sp, flt, piece, size, f...]
where the time goes in v4:
time: 36.1 us; the launch traced here: 36 us
  Pallas kernels  32.2 us (89%)
  local copies, waits for them, and re-layouts  3.13 us (9%)
  between operations  0.65 us (2%)
    pallas_call x1, Pallas kernels, per_device(): pl.pallas_call(functools.partial(backward_kernel, sp, flt, piece, size, f...  32.2 us
    unnamed x4, local copies, waits for them, and re-layouts  1.92 us
    transpose x1, local copies, waits for them, and re-layouts, per_device(): grad_out[:, 0].transpose(1, 0, 2)  1.21 us

profile of v4, /device:TPU:1, one launch (start us, length us, event | category | flops | bytes accessed | tf_op | source)
XLA Modules:
  0.0 36.0 jit_solution(1690646534101545358)
XLA Ops:
  0.6 0.0 copy-start
  0.6 1.2 %copy_bitcast_fusion = (f32[2,64,512]{2,1,0:T(8,128)S(1)}, f32[2,64,512]{2,1,0:T(8,128)S(1)}) fusion(f32[64,1,2,512]{3,2,1,0:T(2,128)} %param.4, f32[64,1,2,512]{3,2,1,0:T(2,128)} %param.3), kind=kLoop, calls=%fused_computation | loop fusion | bytes 1048576 | tf_op jit(solution)/shard_map/transpose | solution.py:419
  1.9 0.1 copy-done
  2.0 32.2 %shard_map.50 = (f32[2,64,512]{2,1,0:T(8,128)S(1)}, f32[27,64,64]{2,1,0:T(8,128)S(1)}) custom-call(f32[2,64,512]{2,1,0:T(8,128)S(1)} %get-tuple-element.9.acts, f32[2,64,512]{2,1,0:T(8,128)S(1)} %get-tuple-element.8.grad, f32[27,64,64]{2,1,0:T(8,128)S(1)} %bitcast.14), custom_call_target="tpu_custom_call" | custom-call | tf_op jit(solution)/shard_map/pallas_call | solution.py:390
  34.1 0.9 %copy.7 = f32[64,1,2,512]{3,2,1,0:T(2,128)} copy(f32[64,1,2,512]{3,0,2,1:T(8,128)S(1)} %bitcast.15) | data formatting | bytes 524288
  35.1 0.9 %copy.11 = f32[3,3,3,64,64]{4,3,2,1,0:T(8,128)} copy(f32[3,3,3,64,64]{4,3,2,1,0:T(8,128)S(1)} %bitcast.13) | data formatting | bytes 884736
Async XLA Ops:
  0.6 1.3 %copy-start = (f32[3,3,3,64,64]{4,3,2,1,0:T(8,128)S(1)}, f32[3,3,3,64,64]{4,3,2,1,0:T(8,128)}, u32[]{:S(2)}) copy-start(f32[3,3,3,64,64]{4,3,2,1,0:T(8,128)} %param.5) | copy-start | bytes 1327108

commit v5 on v2

--- a/solution.py
+++ b/solution.py
@@ -14,12 +14,12 @@
 
 class Group:
     def __init__(self, sp, flt):
-        self.flt, self.count = flt, sp * flt
+        self.sp, self.count = sp, sp * flt
         self.core = lax.axis_index("rep")
-        self.chip = lax.axis_index("sp") * flt + lax.axis_index("flt")
+        self.chip = lax.axis_index("flt") * sp + lax.axis_index("sp")
 
     def peer(self, chip):
-        return {"sp": chip // self.flt, "flt": chip % self.flt}
+        return {"sp": chip % self.sp, "flt": chip // self.sp}
 
     def partner(self):
         return {"rep": 1 - self.core}
@@ -117,8 +117,8 @@
     def finish():
         each(count - 1, add_arrived)
         total[rows(core * half + chip * piece), :] = held[rows(chip * piece), :]
+        pass_on(chip, core).start()
         each(count - 1, lambda k: gather(group.after(k), chip).start())
-        pass_on(chip, core).start()
         each(count - 1, forward)
         each(count, lambda k: pass_on(k, 1 - core).wait_recv())
         each(count, lambda k: to_partner(k).wait_send())

time: 35 us -> 34.9 us (level)
  no operation moved by 1% of the time
where the time goes in v5:
time: 34.9 us; the launch traced here: 34.7 us
  Pallas kernels  31 us (89%)
  local copies, waits for them, and re-layouts  3.13 us (9%)
  between operations  0.65 us (2%)
    pallas_call x1, Pallas kernels, per_device(): pl.pallas_call(functools.partial(backward_kernel, sp, flt, piece, size, f...  31 us
    unnamed x4, local copies, waits for them, and re-layouts  1.92 us
    transpose x1, local copies, waits for them, and re-layouts, per_device(): grad_out[:, 0].transpose(1, 0, 2)  1.21 us

profile of v5, /device:TPU:1, one launch (start us, length us, event | category | flops | bytes accessed | tf_op | source)
XLA Modules:
  0.0 34.7 jit_solution(6470518755090230671)
XLA Ops:
  0.6 0.0 copy-start
  0.6 1.2 %copy_bitcast_fusion = (f32[2,64,512]{2,1,0:T(8,128)S(1)}, f32[2,64,512]{2,1,0:T(8,128)S(1)}) fusion(f32[64,1,2,512]{3,2,1,0:T(2,128)} %param.4, f32[64,1,2,512]{3,2,1,0:T(2,128)} %param.3), kind=kLoop, calls=%fused_computation | loop fusion | bytes 1048576 | tf_op jit(solution)/shard_map/transpose | solution.py:414
  1.9 0.1 copy-done
  2.0 31.0 %shard_map.50 = (f32[2,64,512]{2,1,0:T(8,128)S(1)}, f32[27,64,64]{2,1,0:T(8,128)S(1)}) custom-call(f32[2,64,512]{2,1,0:T(8,128)S(1)} %get-tuple-element.9.acts, f32[2,64,512]{2,1,0:T(8,128)S(1)} %get-tuple-element.8.grad, f32[27,64,64]{2,1,0:T(8,128)S(1)} %bitcast.14), custom_call_target="tpu_custom_call" | custom-call | tf_op jit(solution)/shard_map/pallas_call | solution.py:385
  32.9 0.9 %copy.7 = f32[64,1,2,512]{3,2,1,0:T(2,128)} copy(f32[64,1,2,512]{3,0,2,1:T(8,128)S(1)} %bitcast.15) | data formatting | bytes 524288
  33.8 0.9 %copy.11 = f32[3,3,3,64,64]{4,3,2,1,0:T(8,128)} copy(f32[3,3,3,64,64]{4,3,2,1,0:T(8,128)S(1)} %bitcast.13) | data formatting | bytes 884736
Async XLA Ops:
  0.6 1.3 %copy-start = (f32[3,3,3,64,64]{4,3,2,1,0:T(8,128)S(1)}, f32[3,3,3,64,64]{4,3,2,1,0:T(8,128)}, u32[]{:S(2)}) copy-start(f32[3,3,3,64,64]{4,3,2,1,0:T(8,128)} %param.5) | copy-start | bytes 1327108
